TPU v7x, 128 devices: a whole 4x4x4 slice. The times are simulated.
128 devices in a mesh: grid: 16 (over y, z_hi, core), band: 8 (over z_lo, x).
Axes of the slice: x: 4, y: 4, z: 4 (z_hi: 2, z_lo: 2; z = z_hi * 2 + z_lo), core: 2. Of those that a mesh axis runs over, the one named last changes fastest.
Arguments:
- orbitals: float32 [256, 96, 16, 128], P('band', 'grid'), may hold values from -6 to 6
- potential: float32 [96, 16, 128], P('grid'), may hold values from -2 to 0.5
- rotation: float32 [256, 256], replicated, may hold values from -0.375 to 0.375
Outputs:
- rotated: float32 [256, 96, 16, 128], P('band', 'grid')
All inputs are finite; a program needn't handle non-finite values.
Results may differ from a plain program's by a relative error of at most 0.000071.
Values sent between devices are 32-bit elements; how exact they have to be, the bound alone decides.
A program may use at most 192 MiB of HBM per device.

v0:
```python
import jax
import jax.numpy as jnp
from jax import lax
from jax.sharding import PartitionSpec as P

DEGREE = 4


stencil_coeffs = (
    12.0 / 7.0,
    -15.0 / 56.0,
    10.0 / 189.0,
    -1.0 / 112.0,
    2.0 / 1925.0,
    -1.0 / 16632.0,
)
centre_coeff = -5369.0 / 1800.0
bound_lower = -2.0
bound_cut = 1.0
bound_upper = 16.0


def padded_2(block, sides, width):
    for axis, dim in sides:
        count = lax.axis_size(axis)
        forward = [(i, i + 1) for i in range(count - 1)]
        forward.append((count - 1, 0))
        backward = [(target, source) for source, target in forward]
        low = lax.ppermute(
            lax.slice_in_dim(block, block.shape[dim] - width, None, axis=dim), axis, forward
        )
        high = lax.ppermute(lax.slice_in_dim(block, 0, width, axis=dim), axis, backward)
        block = jnp.concatenate([low, block, high], axis=dim)
    return block


def apply_hamil(field, potential):
    laplace = 3.0 * centre_coeff * field
    rolled_axes = (2, 3)
    planes = field.shape[1]
    padded = padded_2(field, (("grid", 1),), 6)
    for dist, coeff in enumerate(stencil_coeffs):
        upper = padded[:, 7 + dist : 7 + dist + planes]
        lower = padded[:, 5 - dist : 5 - dist + planes]
        laplace = laplace + coeff * (upper + lower)
    for axis_num in rolled_axes:
        for dist, coeff in enumerate(stencil_coeffs):
            laplace = laplace + coeff * (
                jnp.roll(field, dist + 1, axis=axis_num)
                + jnp.roll(field, -(dist + 1), axis=axis_num)
            )
    return -0.5 * laplace + potential[None] * field


def run_filter(orbitals, potential):
    half_width = (bound_upper - bound_cut) / 2.0
    centre = (bound_upper + bound_cut) / 2.0
    sigma_first = half_width / (bound_lower - centre)
    sigma_now = sigma_first
    previous = orbitals
    current = (apply_hamil(orbitals, potential) - centre * orbitals) * (sigma_first / half_width)
    for degree_step in range(DEGREE - 1):
        sigma_new = 1.0 / (2.0 / sigma_first - sigma_now)
        following = (
            2.0 * sigma_new / half_width * (apply_hamil(current, potential) - centre * current)
            - sigma_now * sigma_new * previous
        )
        previous = current
        current = following
        sigma_now = sigma_new
    return current


def local(orbitals, potential, rotation):
    current = run_filter(orbitals, potential)
    local_bands = current.shape[0]
    first_band = lax.axis_index("band") * local_bands
    my_columns = lax.dynamic_slice_in_dim(rotation, first_band, local_bands, 1)
    return jnp.tensordot(
        my_columns,
        lax.all_gather(current, "band", axis=0, tiled=True),
        axes=(0, 0),
        precision=lax.Precision.HIGHEST,
    )


def solution(mesh):
    in_specs = (P("band", "grid", None, None), P("grid", None, None), P())
    out_specs = P("band", "grid", None, None)
    return jax.shard_map(local, mesh=mesh, in_specs=in_specs, out_specs=out_specs, check_vma=False)
```

profile of v0, /device:TPU:1, one launch (start us, length us, event | category | flops | bytes accessed | tf_op | source)
XLA Modules:
  0.0 512.1 jit_solution(6587315423165682542)
XLA Ops:
  6.5 2.4 copy.5
  8.9 5.1 collective-permute-start.1
  16.1 2.3 fusion.268
  20.7 2.3 fusion.270
  22.9 2.3 fusion.271
  63.5 31.8 %broadcast_multiply_fusion = (f32[32,6,16,128]{3,0,2,1:T(8,128)S(1)}, f32[32,6,16,128]{3,0,2,1:T(8,128)}) fusion(f32[6,16,128]{2,1,0:T(8,128)S(1)} %copy-done.13, f32[32,6,16,6]{3,0,2,1:T(8,128)} %get-tuple-element.198, f32[32,6,16,122]{3,0,2,1:T(8,128)} %get-tuple-element.200, f32[32,6,16,122]{3,0,2,1:T(8,128)} %get-tuple-element.199, ...), kind=kLoop, calls=%fused_computation.290 | loop fusion | flops 33423360 | bytes 61390848 | tf_op jit(solution)/shard_map/mul | solution.py:61
  97.1 2.3 fusion.244
  99.4 2.3 fusion.245
  106.2 2.3 fusion.248
  123.6 2.4 collective-permute-start.2
  134.7 2.3 fusion.252
  141.5 20.3 %collective-permute-done.2 = f32[32,6,16,128]{3,0,2,1:T(8,128)S(1)} collective-permute-done((f32[32,6,16,128]{3,0,2,1:T(8,128)S(1)}, f32[32,6,16,128]{3,0,2,1:T(8,128)S(1)}, u32[]{:S(2)}, u32[]{:S(2)}) %collective-permute-start.2) | collective-permute-done | bytes 1572896 | tf_op jit(solution)/shard_map/ppermute | solution.py:32
  163.4 23.5 %multiply_subtract_fusion.2 = f32[32,6,16,128]{3,0,2,1:T(8,128)S(1)} fusion(f32[32,6,16,128]{3,0,2,1:T(8,128)S(1)} %copy-done.4, f32[32,6,16,6]{3,0,2,1:T(8,128)} %get-tuple-element.148, f32[32,6,16,122]{3,0,2,1:T(8,128)} %get-tuple-element.150, f32[32,6,16,122]{3,0,2,1:T(8,128)} %get-tuple-element.149, f32[32,6,16,6]{3,0,2,1:T(8,128)} %get-tuple-element.147, ...), kind=kLoop, calls=%fused_computation.288 | loop fusion | flops 38141952 | bytes 47235072 | tf_op jit(solution)/shard_map/sub | solution.py:65
  189.8 2.3 fusion.219
  213.6 3.4 collective-permute-start.5
  231.3 20.5 %collective-permute-done.4 = f32[32,6,16,128]{3,0,2,1:T(8,128)S(1)} collective-permute-done((f32[32,6,16,128]{3,0,2,1:T(8,128)S(1)}, f32[32,6,16,128]{3,0,2,1:T(8,128)S(1)}, u32[]{:S(2)}, u32[]{:S(2)}) %collective-permute-start.4) | collective-permute-done | bytes 1572896 | tf_op jit(solution)/shard_map/ppermute | solution.py:32
  253.5 22.9 %multiply_subtract_fusion.1 = f32[32,6,16,128]{3,0,2,1:T(8,128)S(1)} fusion(f32[32,6,16,128]{3,0,2,1:T(8,128)S(1)} %copy-done.4, f32[32,6,16,128]{3,0,2,1:T(8,128)S(1)} %multiply_subtract_fusion.2, f32[32,6,16,6]{3,0,2,1:T(8,128)S(1)} %get-tuple-element.100, f32[32,6,16,122]{3,0,2,1:T(8,128)} %get-tuple-element.102, ...), kind=kLoop, calls=%fused_computation.287 | loop fusion | flops 38141952 | bytes 45662208 | tf_op jit(solution)/shard_map/sub | solution.py:65
  278.8 2.3 fusion.197
  302.5 3.5 collective-permute-start.7
  311.3 2.3 fusion.203
  320.2 17.7 %collective-permute-done.6 = f32[32,6,16,128]{3,0,2,1:T(8,128)S(1)} collective-permute-done((f32[32,6,16,128]{3,0,2,1:T(8,128)S(1)}, f32[32,6,16,128]{3,0,2,1:T(8,128)S(1)}, u32[]{:S(2)}, u32[]{:S(2)}) %collective-permute-start.6) | collective-permute-done | bytes 1572896 | tf_op jit(solution)/shard_map/ppermute | solution.py:32
  340.3 23.7 %multiply_subtract_fusion = f32[32,6,16,128]{3,0,2,1:T(8,128)} fusion(f32[32,6,16,128]{3,0,2,1:T(8,128)S(1)} %multiply_subtract_fusion.2, f32[32,6,16,128]{3,0,2,1:T(8,128)S(1)} %multiply_subtract_fusion.1, f32[32,6,16,6]{3,0,2,1:T(8,128)} %get-tuple-element.52, f32[32,6,16,122]{3,0,2,1:T(8,128)} %get-tuple-element.54, ...), kind=kLoop, calls=%fused_computation.286 | loop fusion | flops 38141952 | bytes 45662208 | tf_op jit(solution)/shard_map/sub | solution.py:65
  364.0 128.6 %all-gather.2.cloned.1.call-done = f32[256,6,16,128]{3,0,2,1:T(8,128)} async-done(((f32[32,6,16,128]{3,0,2,1:T(8,128)}), f32[256,6,16,128]{3,0,2,1:T(8,128)}) %all-gather.2.cloned.1.call-update) | async-done | bytes 12582928 | tf_op jit(solution)/shard_map/all_gather | solution.py:81
  492.5 10.2 %fusion.179 = f32[32,6,16,128]{3,0,2,1:T(8,128)S(1)} fusion(f32[256,6,16,128]{3,0,2,1:T(8,128)} %all-gather.2.cloned.1.call-done, f32[256,256]{1,0:T(8,128)S(1)} %copy-done, s32[]{:T(128)S(6)} %select_n.3), kind=kOutput, calls=%fused_computation.291 | convolution fusion | flops 1207959552 | bytes 14286852 | tf_op jit(solution)/shard_map/dot_general | solution.py:79
  (130 shorter events, 159.3 us)
Async XLA Ops:
  6.5 486.0 %copy-start = (f32[256,256]{1,0:T(8,128)S(1)}, f32[256,256]{1,0:T(8,128)}, u32[]{:S(2)}) copy-start(f32[256,256]{1,0:T(8,128)} %param.5) | copy-start | bytes 786436
  6.5 486.0 %all-gather.2.cloned.1.call-start = ((), (), s32[]{:S(2)}) async-start(), calls=%async_computation | async-start | bytes 14155776 | tf_op jit(solution)/shard_map/all_gather | solution.py:81
  8.9 48.4 %collective-permute-start.1 = (f32[32,6,16,128]{3,0,2,1:T(8,128)S(1)}, f32[32,6,16,128]{3,0,2,1:T(8,128)S(1)}, u32[]{:S(2)}, u32[]{:S(2)}) collective-permute-start(f32[32,6,16,128]{3,0,2,1:T(8,128)S(1)} %copy.5), channel_id=1, source_target_pairs={{0,8},{8,16},{16,24},{24,32},{32,40},{40,48},{48,56},{56,64},{64,7... | collective-permute-start | bytes 4718600 | tf_op jit(solution)/shard_map/ppermute | solution.py:29
  14.0 46.2 %collective-permute-start = (f32[32,6,16,128]{3,0,2,1:T(8,128)S(1)}, f32[32,6,16,128]{3,0,2,1:T(8,128)S(1)}, u32[]{:S(2)}, u32[]{:S(2)}) collective-permute-start(f32[32,6,16,128]{3,0,2,1:T(8,128)S(1)} %copy.5), channel_id=1, source_target_pairs={{8,0},{16,8},{24,16},{32,24},{40,32},{48,40},{56,48},{64,56},{72,6... | collective-permute-start | bytes 4718600 | tf_op jit(solution)/shard_map/ppermute | solution.py:32
  48.3 1.7 copy-start.13
  57.3 2.0 copy-start.3
  57.3 1.1 copy-start.5
  60.2 1.7 copy-start.1
  60.2 2.1 copy-start.6
  61.9 1.6 copy-start.2
  123.6 38.2 %collective-permute-start.2 = (f32[32,6,16,128]{3,0,2,1:T(8,128)S(1)}, f32[32,6,16,128]{3,0,2,1:T(8,128)S(1)}, u32[]{:S(2)}, u32[]{:S(2)}) collective-permute-start(f32[32,6,16,128]{3,0,2,1:T(8,128)S(1)} %get-tuple-element.5), channel_id=1, source_target_pairs={{8,0},{16,8},{24,16},{32,24},{40,32},{48,40},{56,48},{64,56},{72,6... | collective-permute-start | bytes 4718600 | tf_op jit(solution)/shard_map/ppermute | solution.py:32
  126.0 35.8 %collective-permute-start.3 = (f32[32,6,16,128]{3,0,2,1:T(8,128)S(1)}, f32[32,6,16,128]{3,0,2,1:T(8,128)S(1)}, u32[]{:S(2)}, u32[]{:S(2)}) collective-permute-start(f32[32,6,16,128]{3,0,2,1:T(8,128)S(1)} %get-tuple-element.5), channel_id=1, source_target_pairs={{0,8},{8,16},{16,24},{24,32},{32,40},{40,48},{48,56},{56,64},{64,7... | collective-permute-start | bytes 4718600 | tf_op jit(solution)/shard_map/ppermute | solution.py:29
  139.3 24.2 %copy-start.4 = (f32[32,6,16,128]{3,0,2,1:T(8,128)S(1)}, f32[32,6,16,128]{3,0,2,1:T(8,128)}, u32[]{:S(2)}) copy-start(f32[32,6,16,128]{3,0,2,1:T(8,128)} %get-tuple-element.6) | copy-start | bytes 4718596
  161.8 1.1 copy-start.7
  161.8 1.6 copy-start.10
  213.6 38.2 %collective-permute-start.4 = (f32[32,6,16,128]{3,0,2,1:T(8,128)S(1)}, f32[32,6,16,128]{3,0,2,1:T(8,128)S(1)}, u32[]{:S(2)}, u32[]{:S(2)}) collective-permute-start(f32[32,6,16,128]{3,0,2,1:T(8,128)S(1)} %multiply_subtract_fusion.2), channel_id=1, source_target_pairs={{8,0},{16,8},{24,16},{32,24},{40,32},{48,40},{56,48},{64,56},{72,6... | collective-permute-start | bytes 4718600 | tf_op jit(solution)/shard_map/ppermute | solution.py:32
  213.6 38.2 %collective-permute-start.5 = (f32[32,6,16,128]{3,0,2,1:T(8,128)S(1)}, f32[32,6,16,128]{3,0,2,1:T(8,128)S(1)}, u32[]{:S(2)}, u32[]{:S(2)}) collective-permute-start(f32[32,6,16,128]{3,0,2,1:T(8,128)S(1)} %multiply_subtract_fusion.2), channel_id=1, source_target_pairs={{0,8},{8,16},{16,24},{24,32},{32,40},{40,48},{48,56},{56,64},{64,7... | collective-permute-start | bytes 4718600 | tf_op jit(solution)/shard_map/ppermute | solution.py:29
  251.8 1.2 copy-start.9
  251.8 1.7 copy-start.12
  302.5 35.4 %collective-permute-start.6 = (f32[32,6,16,128]{3,0,2,1:T(8,128)S(1)}, f32[32,6,16,128]{3,0,2,1:T(8,128)S(1)}, u32[]{:S(2)}, u32[]{:S(2)}) collective-permute-start(f32[32,6,16,128]{3,0,2,1:T(8,128)S(1)} %multiply_subtract_fusion.1), channel_id=1, source_target_pairs={{8,0},{16,8},{24,16},{32,24},{40,32},{48,40},{56,48},{64,56},{72,6... | collective-permute-start | bytes 4718600 | tf_op jit(solution)/shard_map/ppermute | solution.py:32
  302.5 35.4 %collective-permute-start.7 = (f32[32,6,16,128]{3,0,2,1:T(8,128)S(1)}, f32[32,6,16,128]{3,0,2,1:T(8,128)S(1)}, u32[]{:S(2)}, u32[]{:S(2)}) collective-permute-start(f32[32,6,16,128]{3,0,2,1:T(8,128)S(1)} %multiply_subtract_fusion.1), channel_id=1, source_target_pairs={{0,8},{8,16},{16,24},{24,32},{32,40},{40,48},{48,56},{56,64},{64,7... | collective-permute-start | bytes 4718600 | tf_op jit(solution)/shard_map/ppermute | solution.py:29
  337.9 1.2 copy-start.8
  339.1 1.1 copy-start.11
Sparse Core Ops, SparseCore 0:
  364.1 128.4 all-gather.1
where the time goes:
time: 520 us; the launch traced here: 512 us
  waiting for transfers between devices  187 us (36%)
  local copies, waits for them, and re-layouts  183 us (35%)
  other arithmetic  103 us (20%)
  starting transfers between devices  15.4 us (3%)
  between operations  14 us (3%)
  matrix products  10.2 us (2%)
    slice x96, local copies, waits for them, and re-layouts, apply_hamil(): jnp.roll(field, dist + 1, axis=axis_num)  167 us
    all_gather x1, waiting for transfers between devices, local(): lax.all_gather(current, 'band', axis=0, tiled=True)  129 us
    sub x3, other arithmetic, run_filter(): 2.0 * sigma_new / half_width  70.1 us
    ppermute x4, waiting for transfers between devices, padded_2(): lax.ppermute(lax.slice_in_dim(block, 0, width, axis=dim), axis, backward)  58.5 us
    mul x1, other arithmetic, run_filter(): (apply_hamil(orbitals, potential) - centre * orbitals) * (sigma_first / h...  31.8 us
    unnamed x31, local copies, waits for them, and re-layouts  14 us
    ppermute x4, starting transfers between devices, padded_2(): lax.ppermute(lax.slice_in_dim(block, block.shape[dim] - width, None, axis...  13 us
  transfers between devices with their start and end apart: 9, of which 4 were waited for; matrix products, arithmetic and copies ran while one was open for 17% of the time, Pallas kernels for 0%

commit v1 on v0

v1 whole, which is shorter than its diff:
```python
import functools

import jax
import jax.numpy as jnp
from jax import lax
from jax.experimental import pallas as pl
from jax.experimental.pallas import tpu as pltpu
from jax.sharding import PartitionSpec as P

MESH = pl.DeviceIdType.MESH
DEGREE = 4
NB, NX, NY, NZ = 256, 96, 16, 128
GRID, BAND = 16, 8
SLAB = NX // GRID * NY
CELL = NX * NY
XL = 12
PAD = 6

stencil_coeffs = (12.0 / 7.0, -15.0 / 56.0, 10.0 / 189.0, -1.0 / 112.0, 2.0 / 1925.0, -1.0 / 16632.0)
centre_coeff = -5369.0 / 1800.0
bound_lower = -2.0
bound_cut = 1.0
bound_upper = 16.0
HALF = (bound_upper - bound_cut) / 2.0
CENTRE = (bound_upper + bound_cut) / 2.0


def step_factors():
    first = HALF / (bound_lower - CENTRE)
    now, out = first, [(first / HALF, 0.0)]
    for _ in range(DEGREE - 1):
        new = 1.0 / (2.0 / first - now)
        out.append((2.0 * new / HALF, now * new))
        now = new
    return out


def split(value):
    high = value.astype(jnp.bfloat16)
    return high, (value - high.astype(jnp.float32)).astype(jnp.bfloat16)


def tile_count(core, band):
    return 1 + (band + core) % 2


def tile_start(core, band):
    return 3 * (band // 2) + (band % 2) * (1 + core)


def kernel(orb, pot, rot, out, fin, fo, pbuf, w, e0, e1, mb, ob, rh, rl, cz,
           p_send, p_recv, s_send, s_recv, f_send, f_recv, m_send, m_recv, l_sem):
    g, b = lax.axis_index("grid"), lax.axis_index("band")
    y, zhi, core = g // 4, g // 2 % 2, g % 2
    zlo, x = b // 4, b % 4
    z = zhi * 2 + zlo
    cnt, first_tile = tile_count(core, b), tile_start(core, b)

    def grid_of(yy, zh, cc):
        return yy * 4 + zh * 2 + cc

    barrier = pltpu.get_barrier_semaphore()

    def greet(k, carry):
        t = lax.rem(g * BAND + b + k, GRID * BAND)
        pl.semaphore_signal(barrier, inc=1, device_id=(t // BAND, t % BAND), device_id_type=MESH)
        return carry

    lax.fori_loop(1, GRID * BAND, greet, 0)
    pl.semaphore_wait(barrier, GRID * BAND - 1)

    def pot_y(k, carry):
        pltpu.make_async_remote_copy(
            src_ref=pot, dst_ref=pbuf.at[y, zhi, core], send_sem=p_send.at[0], recv_sem=p_recv.at[0],
            device_id=(grid_of((y + 1 + (k + 1) % 3) % 4, zhi, core), b), device_id_type=MESH).start()
        return carry

    lax.fori_loop(0, 3, pot_y, 0)
    own_pot = pltpu.make_async_copy(pot, pbuf.at[y, zhi, core], l_sem.at[0])
    own_pot.start()

    def orb_out(h):
        def one(k, carry):
            dy, dz, dc = (2 + k // 4) % 4, 1 - k // 2 % 2, k % 2
            t = grid_of((y + dy) % 4, (zhi + dz) % 2, (core + dc) % 2)
            row = pl.multiple_of(g * SLAB, SLAB)

            @pl.when(k != 10)
            def _():
                pltpu.make_async_remote_copy(
                    src_ref=orb.at[h * GRID + t], dst_ref=fin.at[h, pl.ds(row, SLAB)],
                    send_sem=s_send.at[h], recv_sem=s_recv.at[h],
                    device_id=(t, b), device_id_type=MESH).start()

            @pl.when(k == 10)
            def _():
                pltpu.make_async_copy(
                    orb.at[h * GRID + g], fin.at[h, pl.ds(row, SLAB)], l_sem.at[1 + h]).start()
            return carry

        lax.fori_loop(0, GRID, one, 0)

    orb_out(0)

    own_pot.wait()
    three = pbuf.at[pl.ds(0, 3), 0, 0]
    pltpu.make_async_copy(three, three, p_recv.at[0]).wait()
    far = (grid_of(y, 1 - zhi, core), (1 - zlo) * 4 + x)
    copy2 = pltpu.make_async_remote_copy(
        src_ref=pbuf.at[:, zhi, core], dst_ref=pbuf.at[:, zhi, core],
        send_sem=p_send.at[1], recv_sem=p_recv.at[1], device_id=far, device_id_type=MESH)
    copy2.start()
    orb_out(1)

    turned = rot[...].T
    high, low = split(turned)
    rh[...] = high
    rl[...] = low
    row = lax.broadcasted_iota(jnp.int32, (NZ, NZ), 0)
    col = lax.broadcasted_iota(jnp.int32, (NZ, NZ), 1)
    away = jnp.abs(row - col)
    away = jnp.minimum(away, NZ - away)
    circ = jnp.zeros((NZ, NZ), jnp.float32)
    for dist, coeff in enumerate(stencil_coeffs):
        circ = jnp.where(away == dist + 1, -0.5 * coeff, circ)
    high, low = split(circ)
    cz[0:NZ, 0:NZ] = high
    cz[NZ:2 * NZ, 0:NZ] = high
    cz[0:NZ, NZ:2 * NZ] = low
    cz[NZ:2 * NZ, NZ:2 * NZ] = jnp.zeros((NZ, NZ), jnp.bfloat16)

    copy2.wait_recv()
    copy3 = pltpu.make_async_remote_copy(
        src_ref=pbuf.at[:, :, core], dst_ref=pbuf.at[:, :, core],
        send_sem=p_send.at[2], recv_sem=p_recv.at[2],
        device_id=(grid_of(y, zhi, 1 - core), b), device_id_type=MESH)
    copy3.start()
    copy3.wait_recv()
    flat = pbuf.reshape(CELL, NZ)

    def fill_w(xl, carry):
        for yy in range(NY):
            w[xl, yy] = flat[pl.ds(xl * NY + yy, 8, stride=XL * NY), :] - (CENTRE + 1.5 * centre_coeff)
        return carry

    lax.fori_loop(0, XL, fill_w, 0)

    def put(ref, xl, half, value):
        ref[xl + PAD] = value
        if half:
            ref[xl - PAD] = pltpu.roll(value, 1, 1)
        else:
            ref[xl + PAD + XL] = pltpu.roll(value, 7, 1)

    def hamil(src, xl):
        c = src[xl + PAD]
        high, low = split(c.reshape(NY * 8, NZ))
        zz = jnp.dot(jnp.concatenate([high, low], axis=1), cz[...], preferred_element_type=jnp.float32)
        acc = (zz[:, :NZ] + zz[:, NZ:]).reshape(NY, 8, NZ) + w[xl] * c
        for dist, coeff in enumerate(stencil_coeffs):
            d = dist + 1
            ring = jnp.concatenate([c[d:], c[:d]], axis=0) + jnp.concatenate([c[NY - d:], c[:NY - d]], axis=0)
            acc = acc + (-0.5 * coeff) * (ring + (src[xl + PAD + d] + src[xl + PAD - d]))
        return acc

    factors = step_factors()

    def one_band(h, carry):
        row = pl.multiple_of(g * SLAB, SLAB)
        pltpu.make_async_copy(orb.at[h * GRID + g], fin.at[h, pl.ds(row, SLAB)], l_sem.at[1 + h]).wait()
        most = fin.at[h, pl.ds(0, CELL - SLAB)]
        pltpu.make_async_copy(most, most, s_recv.at[h]).wait()
        landed, leave = fin.at[h], fo.at[h]
        for half in range(2):
            def load(i, c):
                xl = i + 6 * half
                rows = [landed[pl.ds(xl * NY + yy, 8, stride=XL * NY), :] for yy in range(NY)]
                put(e0, xl, half, jnp.stack(rows, axis=0))
                return c
            lax.fori_loop(0, 6, load, 0)
        for step, (a, prev) in enumerate(factors):
            src, dst = (e0, e1) if step % 2 == 0 else (e1, e0)
            for half in range(2):
                def plane(i, c):
                    xl = i + 6 * half
                    value = a * hamil(src, xl)
                    if step:
                        value = value - prev * dst[xl + PAD]
                    if step < DEGREE - 1:
                        put(dst, xl, half, value)
                    else:
                        for yy in range(NY):
                            leave[pl.ds(xl * NY + yy, 8, stride=XL * NY), :] = value[yy]
                    return c
                lax.fori_loop(0, 6, plane, 0)

        band_row = pl.multiple_of((32 * b + 16 * h + g) * 16, 16)
        for tile in range(2):
            def give(k, c):
                for dc in (1, 0):
                    yy, zz, xx = (y + 2 + k // 16) % 4, (z + 2 + k // 4) % 4, (x + 2 + k) % 4
                    cc, bb = (core + dc) % 2, zz % 2 * 4 + xx
                    gg = grid_of(yy, zz // 2, cc)
                    src_row = pl.multiple_of(gg * SLAB + (tile_start(cc, bb) + tile) * 8, 8)
                    send = pltpu.make_async_remote_copy(
                        src_ref=leave.at[pl.ds(src_row, 8)],
                        dst_ref=mb.at[pl.ds(pl.multiple_of(band_row + tile * 8, 8), 8)],
                        send_sem=f_send, recv_sem=f_recv.at[tile], device_id=(gg, bb), device_id_type=MESH)
                    wanted = tile_count(cc, bb) > tile if tile else True
                    if dc == 0:
                        wanted = jnp.logical_and(wanted, k != 42)
                    if wanted is True:
                        send.start()
                    else:
                        pl.when(wanted)(send.start)
                return c
            lax.fori_loop(0, 64, give, 0)

            def keep():
                own_row = pl.multiple_of(g * SLAB + (first_tile + tile) * 8, 8)
                own = pltpu.make_async_copy(
                    leave.at[pl.ds(own_row, 8)],
                    mb.at[pl.ds(pl.multiple_of(band_row + tile * 8, 8), 8)], l_sem.at[3])
                own.start()
                own.wait()
            if tile:
                pl.when(cnt > tile)(keep)
            else:
                keep()
        return carry

    lax.fori_loop(0, 2, one_band, 0)

    whole = mb.at[pl.ds(0, 254 * 8)]
    blocks = ob.reshape(NB, 16, NZ)

    def home(t):
        return pl.ds(pl.multiple_of((first_tile + t) * 8, 8), 8)

    def tile_work(tile):
        pltpu.make_async_copy(whole, whole, f_recv.at[tile]).wait()

        def pair(r, c):
            at = tile * 8 + 2 * r
            rows = [mb[pl.ds(at + i, NB, stride=16), :] for i in range(2)]
            high, low = split(jnp.concatenate(rows, axis=1))
            res = jnp.dot(rh[...], high, preferred_element_type=jnp.float32)
            res = res + (jnp.dot(rh[...], low, preferred_element_type=jnp.float32)
                         + jnp.dot(rl[...], high, preferred_element_type=jnp.float32))
            for i in range(2):
                ob[pl.ds(at + i, NB, stride=16), :] = res[:, i * NZ:(i + 1) * NZ]
            return c
        lax.fori_loop(0, 4, pair, 0)

        def give(k, c):
            t = lax.rem(b + k, BAND)
            pltpu.make_async_remote_copy(
                src_ref=blocks.at[pl.ds(t * 32, 32), pl.ds(tile * 8, 8)], dst_ref=out.at[:, home(tile)],
                send_sem=m_send, recv_sem=m_recv, device_id=(g, t), device_id_type=MESH).start()
            return c
        lax.fori_loop(1, BAND, give, 0)
        pltpu.make_async_copy(
            blocks.at[pl.ds(b * 32, 32), pl.ds(tile * 8, 8)], out.at[:, home(tile)], l_sem.at[4 + tile]).start()

    def own_done(tile):
        pltpu.make_async_copy(
            blocks.at[pl.ds(b * 32, 32), pl.ds(tile * 8, 8)], out.at[:, home(tile)], l_sem.at[4 + tile]).wait()

    tile_work(0)
    pl.when(cnt == 2)(lambda: tile_work(1))

    own_done(0)
    pl.when(cnt == 2)(lambda: own_done(1))
    for n in (1, 2):
        @pl.when(cnt == n)
        def _():
            got = out.at[:, pl.ds(0, (12 - n) * 8)]
            pltpu.make_async_copy(got, got, m_recv).wait()
            sent = blocks.at[pl.ds(0, 224), pl.ds(0, n * 8)]
            pltpu.make_async_copy(sent, sent, m_send).wait()
            sent = fo.at[:, pl.ds(0, (192 - n) * 8)]
            pltpu.make_async_copy(sent, sent, f_send).wait()
    pltpu.make_async_copy(three, three, p_send.at[0]).wait()
    copy2.wait_send()
    copy3.wait_send()
    for h in range(2):
        most = fin.at[h, pl.ds(0, CELL - SLAB)]
        pltpu.make_async_copy(most, most, s_send.at[h]).wait()


def local(orbitals, potential, rotation):
    bands = orbitals.shape[0]
    f32, bf16 = jnp.float32, jnp.bfloat16
    dma = pltpu.SemaphoreType.DMA
    result = pl.pallas_call(
        kernel,
        out_shape=jax.ShapeDtypeStruct((bands, SLAB, NZ), f32),
        in_specs=[pl.BlockSpec(memory_space=pltpu.HBM)] * 2 + [pl.BlockSpec(memory_space=pltpu.VMEM)],
        out_specs=pl.BlockSpec(memory_space=pltpu.HBM),
        scratch_shapes=[
            pltpu.VMEM((2, CELL, NZ), f32),
            pltpu.VMEM((2, CELL, NZ), f32),
            pltpu.VMEM((4, 2, 2, SLAB, NZ), f32),
            pltpu.VMEM((XL, NY, 8, NZ), f32),
            pltpu.VMEM((XL + 2 * PAD, NY, 8, NZ), f32),
            pltpu.VMEM((XL + 2 * PAD, NY, 8, NZ), f32),
            pltpu.VMEM((NB * 16, NZ), f32),
            pltpu.VMEM((NB * 16, NZ), f32),
            pltpu.VMEM((NB, NB), bf16),
            pltpu.VMEM((NB, NB), bf16),
            pltpu.VMEM((2 * NZ, 2 * NZ), bf16),
            dma((3,)), dma((3,)), dma((2,)), dma((2,)), dma, dma((2,)), dma, dma, dma((6,)),
        ],
        compiler_params=pltpu.CompilerParams(
            collective_id=0, has_side_effects=True, vmem_limit_bytes=48 * 2**20),
    )(orbitals.reshape(bands, SLAB, NZ), potential.reshape(SLAB, NZ), rotation)
    return result.reshape(orbitals.shape)


def solution(mesh):
    in_specs = (P("band", "grid", None, None), P("grid", None, None), P())
    out_specs = P("band", "grid", None, None)
    return jax.shard_map(local, mesh=mesh, in_specs=in_specs, out_specs=out_specs, check_vma=False)
```

time: 520 us -> 103 us (0.20); the launches traced: 512 us -> 102 us
  waiting for transfers between devices: 187 us -> 0 us
  local copies, waits for them, and re-layouts: 183 us -> 4.3 us
  other arithmetic: 103 us -> 0 us
  Pallas kernels: 0 us -> 97.7 us
  starting transfers between devices: 15.4 us -> 0 us
  between operations: 14 us -> 0.01 us
  matrix products: 10.2 us -> 0 us
    slice x96 -> x0, local copies, waits for them, and re-layouts: 167 us -> none  [apply_hamil(): jnp.roll(field, dist + 1, axis=axis_num)]
    all_gather x1 -> x0, waiting for transfers between devices: 129 us -> none  [local(): lax.all_gather(current, 'band', axis=0, tiled=True)]
    pallas_call x0 -> x1, Pallas kernels: none -> 97.7 us  [local(): pl.pallas_call(kernel, out_shape=jax.ShapeDtypeStruct((bands, SLAB, NZ),...]
    sub x3 -> x0, other arithmetic: 70.1 us -> none  [run_filter(): 2.0 * sigma_new / half_width]
    ppermute x8 -> x0, waiting for transfers between devices: 58.5 us -> none  [the longest x4 58.5 us: padded_2(): lax.ppermute(lax.slice_in_dim(block, 0, width, axis=dim), axis, backward)]
    mul x2 -> x0, other arithmetic: 32.4 us -> none  [the longest x1 31.8 us: run_filter(): (apply_hamil(orbitals, potential) - centre * orbitals) * (sigma_first / h...]
    ppermute x8 -> x0, starting transfers between devices: 15.4 us -> none  [the longest x4 13 us: padded_2(): lax.ppermute(lax.slice_in_dim(block, block.shape[dim] - width, None, axis...]
    dot_general x1 -> x0, matrix products: 10.2 us -> none  [local(): jnp.tensordot(my_columns, lax.all_gather(current, 'band', axis=0, tiled=T...]
  transfers between devices with their start and end apart: 9 -> 0, of which waited for: 4 -> 0; matrix products, arithmetic and copies ran while one was open for 17% -> 0% of each run, Pallas kernels for 0% -> 0%
where the time goes in v1:
time: 103 us; the launch traced here: 102 us
  Pallas kernels  97.7 us (95%)
  local copies, waits for them, and re-layouts  4.3 us (4%)
    pallas_call x1, Pallas kernels, local(): pl.pallas_call(kernel, out_shape=jax.ShapeDtypeStruct((bands, SLAB, NZ),...  97.7 us
    unnamed x7, local copies, waits for them, and re-layouts  4.3 us

profile of v1, /device:TPU:1, one launch (start us, length us, event | category | flops | bytes accessed | tf_op | source)
XLA Modules:
  0.0 102.0 jit_solution(13391272212801793684)
XLA Ops:
  0.0 0.0 copy-start
  0.0 1.4 %copy-done = f32[32,6,16,128]{3,2,1,0:T(8,128)S(1)} copy-done((f32[32,6,16,128]{3,2,1,0:T(8,128)S(1)}, f32[32,6,16,128]{3,2,1,0:T(8,128)}, u32[]{:S(2)}) %copy-start) | copy-done | bytes 1572888
  1.4 0.0 copy-start.1
  1.4 0.9 copy-done.1
  2.4 0.0 copy-start.2
  2.4 0.8 copy-done.2
  3.2 97.7 %shard_map.37 = f32[32,96,128]{2,1,0:T(8,128)S(1)} custom-call(f32[32,96,128]{2,1,0:T(8,128)S(1)} %bitcast.4, f32[96,128]{1,0:T(8,128)S(1)} %bitcast.5, f32[256,256]{1,0:T(8,128)S(1)} %copy-done.1), custom_call_target="tpu_custom_call" | custom-call | tf_op jit(solution)/shard_map/pallas_call | solution.py:295
  100.9 1.1 %copy.5 = f32[32,6,16,128]{3,2,1,0:T(8,128)} copy(f32[32,6,16,128]{3,2,1,0:T(8,128)S(1)} %bitcast.3) | data formatting | bytes 3145728
Async XLA Ops:
  0.0 1.4 %copy-start = (f32[32,6,16,128]{3,2,1,0:T(8,128)S(1)}, f32[32,6,16,128]{3,2,1,0:T(8,128)}, u32[]{:S(2)}) copy-start(f32[32,6,16,128]{3,2,1,0:T(8,128)} %param.3) | copy-start | bytes 4718596
  1.4 0.9 copy-start.1
  2.4 0.8 copy-start.2

commit v2 on v1

v2 whole, which is shorter than its diff:
```python
import functools

import jax
import jax.numpy as jnp
from jax import lax
from jax.experimental import pallas as pl
from jax.experimental.pallas import tpu as pltpu
from jax.sharding import PartitionSpec as P

MESH = pl.DeviceIdType.MESH
DEGREE = 4
NB, NX, NY, NZ = 256, 96, 16, 128
GRID, BAND = 16, 8
SLAB = NX // GRID * NY
CELL = NX * NY
XL = 12
PAD = 6
RUN = 3

stencil_coeffs = (12.0 / 7.0, -15.0 / 56.0, 10.0 / 189.0, -1.0 / 112.0, 2.0 / 1925.0, -1.0 / 16632.0)
centre_coeff = -5369.0 / 1800.0
bound_lower = -2.0
bound_cut = 1.0
bound_upper = 16.0
HALF = (bound_upper - bound_cut) / 2.0
CENTRE = (bound_upper + bound_cut) / 2.0


def step_factors():
    first = HALF / (bound_lower - CENTRE)
    now, out = first, [(first / HALF, 0.0)]
    for _ in range(DEGREE - 1):
        new = 1.0 / (2.0 / first - now)
        out.append((2.0 * new / HALF, now * new))
        now = new
    return out


def split(value):
    high = value.astype(jnp.bfloat16)
    return high, (value - high.astype(jnp.float32)).astype(jnp.bfloat16)


def tile_count(core, band):
    return 1 + (band + core) % 2


def tile_start(core, band):
    return 3 * (band // 2) + (band % 2) * (1 + core)


def kernel(orb, pot, rot, out, own, fin, fo, pbuf, w, e0, e1, mb, ob, rv, rh, rl, cz, ready,
           p_send, p_recv, s_send, s_recv, f_send, f_recv, m_send, m_recv, l_sem):
    g, b = lax.axis_index("grid"), lax.axis_index("band")
    y, zhi, core = g // 4, g // 2 % 2, g % 2
    zlo, x = b // 4, b % 4
    z = zhi * 2 + zlo
    cnt, first_tile = tile_count(core, b), tile_start(core, b)
    blocks, landing = ob.reshape(NB, 16, NZ), mb.reshape(NB, 16, NZ)

    def grid_of(yy, zh, cc):
        return yy * 4 + zh * 2 + cc

    orb_in = pltpu.make_async_copy(orb, own, l_sem.at[0])
    orb_in.start()
    pot_in = pltpu.make_async_copy(pot, pbuf.at[y, zhi, core], l_sem.at[1])
    pot_in.start()
    rot_in = pltpu.make_async_copy(rot, rv, l_sem.at[2])
    rot_in.start()

    far = (grid_of(y, 1 - zhi, core), (1 - zlo) * 4 + x)
    barrier = pltpu.get_barrier_semaphore()

    def greet_band(k, carry):
        pl.semaphore_signal(barrier, inc=1, device_id=(g, (b + k) % BAND), device_id_type=MESH)
        return carry

    def greet_grid(k, carry):
        pl.semaphore_signal(barrier, inc=1, device_id=((g + k) % GRID, b), device_id_type=MESH)
        return carry

    lax.fori_loop(1, BAND, greet_band, 0)
    lax.fori_loop(1, GRID, greet_grid, 0)
    pl.semaphore_signal(barrier, inc=1, device_id=far, device_id_type=MESH)
    pl.semaphore_wait(barrier, BAND + GRID - 1)

    def greet_all(k, carry):
        pl.semaphore_signal(ready, inc=1, device_id=(g, (b + k) % BAND), device_id_type=MESH)
        return carry

    orb_in.wait()

    def spread(tile):
        def one(k, carry):
            t = (zlo + 1 + k // 4) % 2 * 4 + (x + 2 + k) % 4
            rows = pl.ds(pl.multiple_of((tile_start(core, t) + tile) * 8, 8), 8)

            @pl.when(jnp.logical_and(k != 6, tile_count(core, t) > tile))
            def _():
                pltpu.make_async_remote_copy(
                    src_ref=own.at[:, rows], dst_ref=landing.at[pl.ds(b * 32, 32), pl.ds(tile * 8, 8)],
                    send_sem=s_send, recv_sem=s_recv.at[tile], device_id=(g, t), device_id_type=MESH).start()
            return carry

        lax.fori_loop(0, BAND, one, 0)

    def mine(tile):
        rows = pl.ds(pl.multiple_of((first_tile + tile) * 8, 8), 8)
        return pltpu.make_async_copy(
            own.at[:, rows], landing.at[pl.ds(b * 32, 32), pl.ds(tile * 8, 8)], l_sem.at[3 + tile])

    spread(0)
    mine(0).start()
    spread(1)
    pl.when(cnt == 2)(lambda: mine(1).start())
    lax.fori_loop(1, BAND, greet_all, 0)

    pot_in.wait()

    def pot_y(k, carry):
        pltpu.make_async_remote_copy(
            src_ref=pbuf.at[y, zhi, core], dst_ref=pbuf.at[y, zhi, core],
            send_sem=p_send.at[0], recv_sem=p_recv.at[0],
            device_id=(grid_of((y + 1 + (k + 1) % 3) % 4, zhi, core), b), device_id_type=MESH).start()
        return carry

    lax.fori_loop(0, 3, pot_y, 0)

    rot_in.wait()
    high, low = split(rv[...].T)
    rh[...] = high
    rl[...] = low
    row = lax.broadcasted_iota(jnp.int32, (NZ, NZ), 0)
    col = lax.broadcasted_iota(jnp.int32, (NZ, NZ), 1)
    away = jnp.abs(row - col)
    away = jnp.minimum(away, NZ - away)
    circ = jnp.zeros((NZ, NZ), jnp.float32)
    for dist, coeff in enumerate(stencil_coeffs):
        circ = jnp.where(away == dist + 1, -0.5 * coeff, circ)
    high, low = split(circ)
    cz[0:NZ, 0:NZ] = high
    cz[NZ:2 * NZ, 0:NZ] = high
    cz[0:NZ, NZ:2 * NZ] = low
    cz[NZ:2 * NZ, NZ:2 * NZ] = jnp.zeros((NZ, NZ), jnp.bfloat16)

    three = pbuf.at[pl.ds(0, 3), 0, 0]
    pltpu.make_async_copy(three, three, p_recv.at[0]).wait()
    copy2 = pltpu.make_async_remote_copy(
        src_ref=pbuf.at[:, zhi, core], dst_ref=pbuf.at[:, zhi, core],
        send_sem=p_send.at[1], recv_sem=p_recv.at[1], device_id=far, device_id_type=MESH)
    copy2.start()
    copy2.wait_recv()
    copy3 = pltpu.make_async_remote_copy(
        src_ref=pbuf.at[:, :, core], dst_ref=pbuf.at[:, :, core],
        send_sem=p_send.at[2], recv_sem=p_recv.at[2],
        device_id=(grid_of(y, zhi, 1 - core), b), device_id_type=MESH)
    copy3.start()
    pl.semaphore_wait(ready, BAND - 1)

    def rotate(tile):
        mine(tile).wait()
        got = landing.at[pl.ds(0, NB - 32), pl.ds(0, 8)]
        pltpu.make_async_copy(got, got, s_recv.at[tile]).wait()

        def pair(r, c):
            at = tile * 8 + 2 * r
            rows = [mb[pl.ds(at + i, NB, stride=16), :] for i in range(2)]
            high, low = split(jnp.concatenate(rows, axis=1))
            res = jnp.dot(rh[...], high, preferred_element_type=jnp.float32)
            res = res + (jnp.dot(rh[...], low, preferred_element_type=jnp.float32)
                         + jnp.dot(rl[...], high, preferred_element_type=jnp.float32))
            for i in range(2):
                ob[pl.ds(at + i, NB, stride=16), :] = res[:, i * NZ:(i + 1) * NZ]
            return c
        lax.fori_loop(0, 4, pair, 0)

    def gather(h, tile, tiles):
        place = pl.ds(pl.multiple_of(g * SLAB + (first_tile + tile) * 8, 8), 8 * tiles)

        def rows(gg, bb):
            return ob.at[pl.ds(pl.multiple_of((32 * bb + 16 * h + gg) * 16 + tile * 8, 8), 8 * tiles)]

        def one(k, c):
            for dc in (1, 0):
                yy, zz, xx = (y + 2 + k // 16) % 4, (z + 2 + k // 4) % 4, (x + 2 + k) % 4
                gg, bb = grid_of(yy, zz // 2, (core + dc) % 2), zz % 2 * 4 + xx
                send = pltpu.make_async_remote_copy(
                    src_ref=rows(gg, bb), dst_ref=fin.at[h, place],
                    send_sem=m_send, recv_sem=m_recv.at[h], device_id=(gg, bb), device_id_type=MESH)
                if dc == 0:
                    pl.when(k != 42)(send.start)
                else:
                    send.start()
            return c
        lax.fori_loop(0, 64, one, 0)
        keep = pltpu.make_async_copy(rows(g, b), fin.at[h, place], l_sem.at[5])
        keep.start()
        keep.wait()

    rotate(0)
    gather(0, 0, 1)

    @pl.when(cnt == 2)
    def _():
        rotate(1)
        gather(0, 1, 1)
        gather(1, 0, 2)

    @pl.when(cnt == 1)
    def _():
        gather(1, 0, 1)

    copy3.wait_recv()
    flat = pbuf.reshape(CELL, NZ)

    def fill_w(xl, carry):
        for yy in range(NY):
            w[xl, yy] = flat[pl.ds(xl * NY + yy, 8, stride=XL * NY), :] - (CENTRE + 1.5 * centre_coeff)
        return carry

    lax.fori_loop(0, XL, fill_w, 0)

    def put(ref, xl, half, value):
        ref[xl + PAD] = value
        if half:
            ref[xl - PAD] = pltpu.roll(value, 1, 1)
        else:
            ref[xl + PAD + XL] = pltpu.roll(value, 7, 1)

    def stencil_xy(src, xl):
        c = src[xl + PAD]
        acc = w[xl] * c
        for dist, coeff in enumerate(stencil_coeffs):
            d = dist + 1
            ring = jnp.concatenate([c[d:], c[:d]], axis=0) + jnp.concatenate([c[NY - d:], c[:NY - d]], axis=0)
            acc = acc + (-0.5 * coeff) * (ring + (src[xl + PAD + d] + src[xl + PAD - d]))
        return acc

    def stencil_z(src, xl):
        high, low = split(src[pl.ds(xl + PAD, RUN)].reshape(RUN * NY * 8, NZ))
        both = jnp.dot(jnp.concatenate([high, low], axis=1), cz[...], preferred_element_type=jnp.float32)
        return (both[:, :NZ] + both[:, NZ:]).reshape(RUN, NY, 8, NZ)

    factors = step_factors()

    def one_band(h, carry):
        for n in (1, 2):
            @pl.when(cnt == n)
            def _():
                most = fin.at[h, pl.ds(0, (192 - n) * 8)]
                pltpu.make_async_copy(most, most, m_recv.at[h]).wait()
        landed, leave = fin.at[h], fo.at[h]
        for half in range(2):
            def load(i, c):
                xl = i + 6 * half
                rows = [landed[pl.ds(xl * NY + yy, 8, stride=XL * NY), :] for yy in range(NY)]
                put(e0, xl, half, jnp.stack(rows, axis=0))
                return c
            lax.fori_loop(0, 6, load, 0)
        for step, (a, prev) in enumerate(factors):
            src, dst = (e0, e1) if step % 2 == 0 else (e1, e0)
            for half in range(2):
                def planes(i, c):
                    along_z = stencil_z(src, i * RUN + 6 * half)
                    for j in range(RUN):
                        xl = i * RUN + j + 6 * half
                        value = a * (stencil_xy(src, xl) + along_z[j])
                        if step:
                            value = value - prev * dst[xl + PAD]
                        if step < DEGREE - 1:
                            put(dst, xl, half, value)
                        else:
                            for yy in range(NY):
                                leave[pl.ds(xl * NY + yy, 8, stride=XL * NY), :] = value[yy]
                    return c
                lax.fori_loop(0, 6 // RUN, planes, 0)

        def home(k, c):
            dy, dz, dc = (2 + k // 4) % 4, 1 - k // 2 % 2, k % 2
            t = grid_of((y + dy) % 4, (zhi + dz) % 2, (core + dc) % 2)
            slab = leave.at[pl.ds(pl.multiple_of(t * SLAB, SLAB), SLAB)]

            @pl.when(k != 10)
            def _():
                pltpu.make_async_remote_copy(
                    src_ref=slab, dst_ref=out.at[h * GRID + g], send_sem=f_send, recv_sem=f_recv,
                    device_id=(t, b), device_id_type=MESH).start()

            @pl.when(k == 10)
            def _():
                pltpu.make_async_copy(slab, out.at[h * GRID + g], l_sem.at[6 + h]).start()
            return c
        lax.fori_loop(0, GRID, home, 0)
        return carry

    lax.fori_loop(0, 2, one_band, 0)

    for h in range(2):
        slab = fo.at[h, pl.ds(pl.multiple_of(g * SLAB, SLAB), SLAB)]
        pltpu.make_async_copy(slab, out.at[h * GRID + g], l_sem.at[6 + h]).wait()
    got = out.at[pl.ds(0, 2 * GRID - 2)]
    pltpu.make_async_copy(got, got, f_recv).wait()
    pltpu.make_async_copy(got, got, f_send).wait()
    for n in (1, 2):
        @pl.when(cnt == n)
        def _():
            sent = own.at[:, pl.ds(0, (12 - n) * 8)]
            pltpu.make_async_copy(sent, sent, s_send).wait()
            sent = mb.at[pl.ds(0, 254 * 8 * n)]
            pltpu.make_async_copy(sent, sent, m_send).wait()
    pltpu.make_async_copy(three, three, p_send.at[0]).wait()
    copy2.wait_send()
    copy3.wait_send()


def local(orbitals, potential, rotation):
    bands = orbitals.shape[0]
    f32, bf16 = jnp.float32, jnp.bfloat16
    dma = pltpu.SemaphoreType.DMA
    result = pl.pallas_call(
        kernel,
        out_shape=jax.ShapeDtypeStruct((bands, SLAB, NZ), f32),
        in_specs=[pl.BlockSpec(memory_space=pltpu.HBM)] * 3,
        out_specs=pl.BlockSpec(memory_space=pltpu.HBM),
        scratch_shapes=[
            pltpu.VMEM((bands, SLAB, NZ), f32),
            pltpu.VMEM((2, CELL, NZ), f32),
            pltpu.VMEM((2, CELL, NZ), f32),
            pltpu.VMEM((4, 2, 2, SLAB, NZ), f32),
            pltpu.VMEM((XL, NY, 8, NZ), f32),
            pltpu.VMEM((XL + 2 * PAD, NY, 8, NZ), f32),
            pltpu.VMEM((XL + 2 * PAD, NY, 8, NZ), f32),
            pltpu.VMEM((NB * 16, NZ), f32),
            pltpu.VMEM((NB * 16, NZ), f32),
            pltpu.VMEM((NB, NB), f32),
            pltpu.VMEM((NB, NB), bf16),
            pltpu.VMEM((NB, NB), bf16),
            pltpu.VMEM((2 * NZ, 2 * NZ), bf16),
            pltpu.SemaphoreType.REGULAR,
            dma((3,)), dma((3,)), dma, dma((2,)), dma, dma, dma, dma((2,)), dma((8,)),
        ],
        compiler_params=pltpu.CompilerParams(
            collective_id=0, has_side_effects=True, vmem_limit_bytes=62 * 2**20),
    )(orbitals.reshape(bands, SLAB, NZ), potential.reshape(SLAB, NZ), rotation)
    return result.reshape(orbitals.shape)


def solution(mesh):
    in_specs = (P("band", "grid", None, None), P("grid", None, None), P())
    out_specs = P("band", "grid", None, None)
    return jax.shard_map(local, mesh=mesh, in_specs=in_specs, out_specs=out_specs, check_vma=False)
```

time: 103 us -> 71.8 us (0.70)
  Pallas kernels: 97.7 us -> 69 us
  local copies, waits for them, and re-layouts: 4.3 us -> 2.66 us
    pallas_call x1, Pallas kernels: 97.7 us -> 69 us  [local(): pl.pallas_call(kernel, out_shape=jax.ShapeDtypeStruct((bands, SLAB, NZ),...]
    unnamed x7 -> x1, local copies, waits for them, and re-layouts: 4.3 us -> 2.66 us
where the time goes in v2:
time: 71.8 us; the launch traced here: 71.7 us
  Pallas kernels  69 us (96%)
  local copies, waits for them, and re-layouts  2.66 us (4%)
    pallas_call x1, Pallas kernels, local(): pl.pallas_call(kernel, out_shape=jax.ShapeDtypeStruct((bands, SLAB, NZ),...  69 us
    unnamed x1, local copies, waits for them, and re-layouts  2.66 us

profile of v2, /device:TPU:1, one launch (start us, length us, event | category | flops | bytes accessed | tf_op | source)
XLA Modules:
  0.0 71.7 jit_solution(2186459478530901878)
XLA Ops:
  0.0 69.0 %shard_map.37 = f32[32,96,128]{2,1,0:T(8,128)} custom-call(f32[32,96,128]{2,1,0:T(8,128)} %bitcast.4, f32[96,128]{1,0:T(8,128)} %bitcast.5, f32[256,256]{1,0:T(8,128)} %rot.1), custom_call_target="tpu_custom_call" | custom-call | tf_op jit(solution)/shard_map/pallas_call | solution.py:320
  69.0 2.7 %copy.5 = f32[32,6,16,128]{3,2,1,0:T(8,128)} copy(f32[32,6,16,128]{3,2,1,0:T(8,128)} %bitcast.3) | data formatting | bytes 3145728

commit v3 on v2

--- a/solution.py
+++ b/solution.py
@@ -15,7 +15,7 @@
 CELL = NX * NY
 XL = 12
 PAD = 6
-RUN = 3
+RUN = 6
 
 stencil_coeffs = (12.0 / 7.0, -15.0 / 56.0, 10.0 / 189.0, -1.0 / 112.0, 2.0 / 1925.0, -1.0 / 16632.0)
 centre_coeff = -5369.0 / 1800.0
@@ -155,6 +155,16 @@
         send_sem=p_send.at[2], recv_sem=p_recv.at[2],
         device_id=(grid_of(y, zhi, 1 - core), b), device_id_type=MESH)
     copy3.start()
+    copy3.wait_recv()
+    flat = pbuf.reshape(CELL, NZ)
+
+    def fill_w(xl, carry):
+        for yy in range(NY):
+            w[xl, yy] = flat[pl.ds(xl * NY + yy, 8, stride=XL * NY), :] - (CENTRE + 1.5 * centre_coeff)
+        return carry
+
+    lax.fori_loop(0, XL, fill_w, 0)
+
     pl.semaphore_wait(ready, BAND - 1)
 
     def rotate(tile):
@@ -180,22 +190,29 @@
         def rows(gg, bb):
             return ob.at[pl.ds(pl.multiple_of((32 * bb + 16 * h + gg) * 16 + tile * 8, 8), 8 * tiles)]
 
-        def one(k, c):
+        def one(first, c, k):
             for dc in (1, 0):
-                yy, zz, xx = (y + 2 + k // 16) % 4, (z + 2 + k // 4) % 4, (x + 2 + k) % 4
+                xy = k // 2 if first == 1 else k
+                dz = (2, 1 + 2 * (k % 2), 0)[first]
+                yy, zz, xx = (y + 2 + xy // 4) % 4, (z + dz) % 4, (x + 2 + xy + xy // 4) % 4
                 gg, bb = grid_of(yy, zz // 2, (core + dc) % 2), zz % 2 * 4 + xx
                 send = pltpu.make_async_remote_copy(
                     src_ref=rows(gg, bb), dst_ref=fin.at[h, place],
-                    send_sem=m_send, recv_sem=m_recv.at[h], device_id=(gg, bb), device_id_type=MESH)
-                if dc == 0:
-                    pl.when(k != 42)(send.start)
+                    send_sem=m_send.at[h], recv_sem=m_recv.at[h], device_id=(gg, bb), device_id_type=MESH)
+                if dc == 0 and first == 2:
+                    pl.when(k != 8)(send.start)
                 else:
                     send.start()
             return c
-        lax.fori_loop(0, 64, one, 0)
+        for first, count in enumerate((16, 32, 16)):
+            lax.fori_loop(0, count, lambda k, c: one(first, c, k), 0)
         keep = pltpu.make_async_copy(rows(g, b), fin.at[h, place], l_sem.at[5])
         keep.start()
         keep.wait()
+
+    def sent_all(h, n):
+        sent = mb.at[pl.ds(0, 127 * 8 * n)]
+        pltpu.make_async_copy(sent, sent, m_send.at[h]).wait()
 
     rotate(0)
     gather(0, 0, 1)
@@ -204,21 +221,13 @@
     def _():
         rotate(1)
         gather(0, 1, 1)
+        sent_all(0, 2)
         gather(1, 0, 2)
 
     @pl.when(cnt == 1)
     def _():
+        sent_all(0, 1)
         gather(1, 0, 1)
-
-    copy3.wait_recv()
-    flat = pbuf.reshape(CELL, NZ)
-
-    def fill_w(xl, carry):
-        for yy in range(NY):
-            w[xl, yy] = flat[pl.ds(xl * NY + yy, 8, stride=XL * NY), :] - (CENTRE + 1.5 * centre_coeff)
-        return carry
-
-    lax.fori_loop(0, XL, fill_w, 0)
 
     def put(ref, xl, half, value):
         ref[xl + PAD] = value
@@ -243,12 +252,35 @@
 
     factors = step_factors()
 
+    def home(h, first, last):
+        def one(k, c):
+            dy, dz, dc = (2 + k // 2 % 4) % 4, 1 - k % 2, 1 - k // 8
+            t = grid_of((y + dy) % 4, (zhi + dz) % 2, (core + dc) % 2)
+            slab = fo.at[h, pl.ds(pl.multiple_of(t * SLAB, SLAB), SLAB)]
+
+            @pl.when(k != 13)
+            def _():
+                pltpu.make_async_remote_copy(
+                    src_ref=slab, dst_ref=out.at[h * GRID + g], send_sem=f_send, recv_sem=f_recv,
+                    device_id=(t, b), device_id_type=MESH).start()
+
+            @pl.when(k == 13)
+            def _():
+                pltpu.make_async_copy(slab, out.at[h * GRID + g], l_sem.at[6 + h]).start()
+            return c
+        lax.fori_loop(first, last, one, 0)
+
     def one_band(h, carry):
         for n in (1, 2):
             @pl.when(cnt == n)
             def _():
                 most = fin.at[h, pl.ds(0, (192 - n) * 8)]
                 pltpu.make_async_copy(most, most, m_recv.at[h]).wait()
+
+        @pl.when(h == 1)
+        def _():
+            home(0, 8, 16)
+
         landed, leave = fin.at[h], fo.at[h]
         for half in range(2):
             def load(i, c):
@@ -275,25 +307,14 @@
                     return c
                 lax.fori_loop(0, 6 // RUN, planes, 0)
 
-        def home(k, c):
-            dy, dz, dc = (2 + k // 4) % 4, 1 - k // 2 % 2, k % 2
-            t = grid_of((y + dy) % 4, (zhi + dz) % 2, (core + dc) % 2)
-            slab = leave.at[pl.ds(pl.multiple_of(t * SLAB, SLAB), SLAB)]
-
-            @pl.when(k != 10)
-            def _():
-                pltpu.make_async_remote_copy(
-                    src_ref=slab, dst_ref=out.at[h * GRID + g], send_sem=f_send, recv_sem=f_recv,
-                    device_id=(t, b), device_id_type=MESH).start()
-
-            @pl.when(k == 10)
-            def _():
-                pltpu.make_async_copy(slab, out.at[h * GRID + g], l_sem.at[6 + h]).start()
-            return c
-        lax.fori_loop(0, GRID, home, 0)
+
+        @pl.when(h == 0)
+        def _():
+            home(0, 0, 8)
         return carry
 
     lax.fori_loop(0, 2, one_band, 0)
+    home(1, 0, GRID)
 
     for h in range(2):
         slab = fo.at[h, pl.ds(pl.multiple_of(g * SLAB, SLAB), SLAB)]
@@ -306,8 +327,7 @@
         def _():
             sent = own.at[:, pl.ds(0, (12 - n) * 8)]
             pltpu.make_async_copy(sent, sent, s_send).wait()
-            sent = mb.at[pl.ds(0, 254 * 8 * n)]
-            pltpu.make_async_copy(sent, sent, m_send).wait()
+            sent_all(1, n)
     pltpu.make_async_copy(three, three, p_send.at[0]).wait()
     copy2.wait_send()
     copy3.wait_send()
@@ -317,6 +337,7 @@
     bands = orbitals.shape[0]
     f32, bf16 = jnp.float32, jnp.bfloat16
     dma = pltpu.SemaphoreType.DMA
+    arrays = orbitals.reshape(bands, SLAB, NZ), potential.reshape(SLAB, NZ), rotation
     result = pl.pallas_call(
         kernel,
         out_shape=jax.ShapeDtypeStruct((bands, SLAB, NZ), f32),
@@ -337,11 +358,11 @@
             pltpu.VMEM((NB, NB), bf16),
             pltpu.VMEM((2 * NZ, 2 * NZ), bf16),
             pltpu.SemaphoreType.REGULAR,
-            dma((3,)), dma((3,)), dma, dma((2,)), dma, dma, dma, dma((2,)), dma((8,)),
+            dma((3,)), dma((3,)), dma, dma((2,)), dma, dma, dma((2,)), dma((2,)), dma((8,)),
         ],
         compiler_params=pltpu.CompilerParams(
-            collective_id=0, has_side_effects=True, vmem_limit_bytes=62 * 2**20),
-    )(orbitals.reshape(bands, SLAB, NZ), potential.reshape(SLAB, NZ), rotation)
+            collective_id=0, has_side_effects=True, vmem_limit_bytes=40 * 2**20),
+    )(*[pltpu.with_memory_space_constraint(value, pltpu.HBM) for value in arrays])
     return result.reshape(orbitals.shape)
 
 

time: 71.8 us -> 67.8 us (0.944)
  Pallas kernels: 69 us -> 66.5 us
  local copies, waits for them, and re-layouts: 2.66 us -> 1.15 us
    pallas_call x1, Pallas kernels: 69 us -> 66.5 us  [local(): pl.pallas_call(kernel, out_shape=jax.ShapeDtypeStruct((bands, SLAB, NZ),...]
    unnamed x1, local copies, waits for them, and re-layouts: 2.66 us -> 1.15 us
where the time goes in v3:
time: 67.8 us; the launch traced here: 67.7 us
  Pallas kernels  66.5 us (98%)
  local copies, waits for them, and re-layouts  1.15 us (2%)
    pallas_call x1, Pallas kernels, local(): pl.pallas_call(kernel, out_shape=jax.ShapeDtypeStruct((bands, SLAB, NZ),...  66.5 us

profile of v3, /device:TPU:1, one launch (start us, length us, event | category | flops | bytes accessed | tf_op | source)
XLA Modules:
  0.0 67.7 jit_solution(262540858927901690)
XLA Ops:
  0.0 66.5 %shard_map.37 = f32[32,96,128]{2,1,0:T(8,128)S(1)} custom-call(f32[32,96,128]{2,1,0:T(8,128)} %bitcast.4, f32[96,128]{1,0:T(8,128)} %bitcast.5, f32[256,256]{1,0:T(8,128)} %rot.1), custom_call_target="tpu_custom_call" | custom-call | tf_op jit(solution)/shard_map/pallas_call | solution.py:341
  66.5 1.1 %copy.5 = f32[32,6,16,128]{3,2,1,0:T(8,128)} copy(f32[32,6,16,128]{3,2,1,0:T(8,128)S(1)} %bitcast.3) | data formatting | bytes 3145728

commit v4 on v3

--- a/solution.py
+++ b/solution.py
@@ -279,7 +279,7 @@
 
         @pl.when(h == 1)
         def _():
-            home(0, 8, 16)
+            home(0, 8 * core, 8 * core + 8)
 
         landed, leave = fin.at[h], fo.at[h]
         for half in range(2):
@@ -306,15 +306,13 @@
                                 leave[pl.ds(xl * NY + yy, 8, stride=XL * NY), :] = value[yy]
                     return c
                 lax.fori_loop(0, 6 // RUN, planes, 0)
-
-
-        @pl.when(h == 0)
-        def _():
-            home(0, 0, 8)
+                if step == DEGREE - 1 and half == 0:
+                    home(h, 8 - 8 * core, 16 - 8 * core)
+
         return carry
 
     lax.fori_loop(0, 2, one_band, 0)
-    home(1, 0, GRID)
+    home(1, 8 * core, 8 * core + 8)
 
     for h in range(2):
         slab = fo.at[h, pl.ds(pl.multiple_of(g * SLAB, SLAB), SLAB)]

time: 67.8 us -> 66.8 us (0.985)
  Pallas kernels: 66.5 us -> 65.5 us
    pallas_call x1, Pallas kernels: 66.5 us -> 65.5 us  [local(): pl.pallas_call(kernel, out_shape=jax.ShapeDtypeStruct((bands, SLAB, NZ),...]
where the time goes in v4:
time: 66.8 us; the launch traced here: 66.7 us
  Pallas kernels  65.5 us (98%)
  local copies, waits for them, and re-layouts  1.15 us (2%)
    pallas_call x1, Pallas kernels, local(): pl.pallas_call(kernel, out_shape=jax.ShapeDtypeStruct((bands, SLAB, NZ),...  65.5 us

profile of v4, /device:TPU:1, one launch (start us, length us, event | category | flops | bytes accessed | tf_op | source)
XLA Modules:
  0.0 66.7 jit_solution(9029190076244126758)
XLA Ops:
  0.0 65.5 %shard_map.37 = f32[32,96,128]{2,1,0:T(8,128)S(1)} custom-call(f32[32,96,128]{2,1,0:T(8,128)} %bitcast.4, f32[96,128]{1,0:T(8,128)} %bitcast.5, f32[256,256]{1,0:T(8,128)} %rot.1), custom_call_target="tpu_custom_call" | custom-call | tf_op jit(solution)/shard_map/pallas_call | solution.py:339
  65.5 1.1 %copy.5 = f32[32,6,16,128]{3,2,1,0:T(8,128)} copy(f32[32,6,16,128]{3,2,1,0:T(8,128)S(1)} %bitcast.3) | data formatting | bytes 3145728

commit v5 on v4

--- a/solution.py
+++ b/solution.py
@@ -206,28 +206,31 @@
             return c
         for first, count in enumerate((16, 32, 16)):
             lax.fori_loop(0, count, lambda k, c: one(first, c, k), 0)
-        keep = pltpu.make_async_copy(rows(g, b), fin.at[h, place], l_sem.at[5])
+        keep = pltpu.make_async_copy(rows(g, b), fin.at[h, place], l_sem.at[(5 + 3 * tile) if h == 0 else 9])
         keep.start()
-        keep.wait()
+        return keep
 
     def sent_all(h, n):
         sent = mb.at[pl.ds(0, 127 * 8 * n)]
         pltpu.make_async_copy(sent, sent, m_send.at[h]).wait()
 
     rotate(0)
-    gather(0, 0, 1)
+    kept = gather(0, 0, 1)
 
     @pl.when(cnt == 2)
     def _():
         rotate(1)
-        gather(0, 1, 1)
+        more = gather(0, 1, 1)
         sent_all(0, 2)
-        gather(1, 0, 2)
+        gather(1, 0, 2).wait()
+        more.wait()
 
     @pl.when(cnt == 1)
     def _():
         sent_all(0, 1)
-        gather(1, 0, 1)
+        gather(1, 0, 1).wait()
+
+    kept.wait()
 
     def put(ref, xl, half, value):
         ref[xl + PAD] = value
@@ -356,7 +359,7 @@
             pltpu.VMEM((NB, NB), bf16),
             pltpu.VMEM((2 * NZ, 2 * NZ), bf16),
             pltpu.SemaphoreType.REGULAR,
-            dma((3,)), dma((3,)), dma, dma((2,)), dma, dma, dma((2,)), dma((2,)), dma((8,)),
+            dma((3,)), dma((3,)), dma, dma((2,)), dma, dma, dma((2,)), dma((2,)), dma((10,)),
         ],
         compiler_params=pltpu.CompilerParams(
             collective_id=0, has_side_effects=True, vmem_limit_bytes=40 * 2**20),

time: 66.8 us -> 66.8 us (level)
  no operation moved by 1% of the time
where the time goes in v5:
time: 66.8 us; the launch traced here: 66.7 us
  Pallas kernels  65.5 us (98%)
  local copies, waits for them, and re-layouts  1.15 us (2%)
    pallas_call x1, Pallas kernels, local(): pl.pallas_call(kernel, out_shape=jax.ShapeDtypeStruct((bands, SLAB, NZ),...  65.5 us

profile of v5, /device:TPU:1, one launch (start us, length us, event | category | flops | bytes accessed | tf_op | source)
XLA Modules:
  0.0 66.7 jit_solution(15646785386040290487)
XLA Ops:
  0.0 65.5 %shard_map.37 = f32[32,96,128]{2,1,0:T(8,128)S(1)} custom-call(f32[32,96,128]{2,1,0:T(8,128)} %bitcast.4, f32[96,128]{1,0:T(8,128)} %bitcast.5, f32[256,256]{1,0:T(8,128)} %rot.1), custom_call_target="tpu_custom_call" | custom-call | tf_op jit(solution)/shard_map/pallas_call | solution.py:342
  65.5 1.1 %copy.5 = f32[32,6,16,128]{3,2,1,0:T(8,128)} copy(f32[32,6,16,128]{3,2,1,0:T(8,128)S(1)} %bitcast.3) | data formatting | bytes 3145728
